TPU v7x, 256 devices: a whole 4x4x8 slice. The times are simulated.
256 devices in a mesh: prow: 8 (over x, core), pcol: 32 (over z, y).
Axes of the slice: x: 4, y: 4, z: 8, core: 2. Of those that a mesh axis runs over, the one named last changes fastest.
Arguments:
- matrix: bfloat16 [4, 8, 512, 1, 32, 512], P(None, 'prow', None, None, 'pcol'), may hold values from -6 to 6
- upper_inv: bfloat16 [2, 512, 512], replicated, may hold values from -4 to 4
- lower_inv: bfloat16 [2, 512, 512], replicated, may hold values from -4 to 4
- solution: bfloat16 [1, 32, 512], P(None, 'pcol'), may hold values from -0.046875 to 0.046875
- right_side: float32 [4, 8, 512], P(None, 'prow'), may hold values from -6 to 6
- diagonal_block_inverses: bfloat16 [1, 8, 512, 512], P(None, 'prow'), may hold values from -0.009765625 to 0.009765625
Outputs:
- updated: bfloat16 [4, 8, 512, 1, 32, 512], P(None, 'prow', None, None, 'pcol')
- residual: float32 [4, 8, 512], P(None, 'prow')
- precond: float32 [8, 512], replicated
All inputs are finite; a program needn't handle non-finite values.
Results may differ from a plain program's by a relative error of at most 0.0085.
Values may be sent and summed in bfloat16 or wider, within the bound.
A program may use at most 128 MiB of HBM per device.

v0:
```python
import jax
import jax.numpy as jnp
from jax import lax
from jax.sharding import PartitionSpec as P

PANELS = 2


def broadcast(value, axis, source):
    kept = jnp.where(lax.axis_index(axis) == source, value, 0).astype(value.dtype)
    return lax.psum(kept, axis)


def shards(matrix, upper_inv, lower_inv, solution, right_side, diagonal_block_inverses):
    rows_blk = matrix.shape[0]
    cols_blk = matrix.shape[3]
    blk_width = matrix.shape[2]
    row_processors = lax.axis_size("prow")
    col_devs = lax.axis_size("pcol")
    col_index = lax.axis_index("pcol")
    base_matrix = matrix.reshape(rows_blk * blk_width, cols_blk * blk_width)
    current = base_matrix
    for section in range(PANELS):
        col_local = section // col_devs
        local_row_block = section // row_processors
        upper_tri = jnp.triu(upper_inv[section])
        lower_tri = jnp.tril(lower_inv[section])
        column = current
        row_band = current[local_row_block * blk_width : (local_row_block + 1) * blk_width, :]
        factored = jnp.dot(column, upper_tri, preferred_element_type=jnp.float32).astype(
            jnp.bfloat16
        )
        left_panel = broadcast(factored, "pcol", section % col_devs)
        top_local = jnp.dot(lower_tri, row_band, preferred_element_type=jnp.float32).astype(
            jnp.bfloat16
        )
        top_panel = broadcast(top_local, "prow", section % row_processors)
        current = (
            current.astype(jnp.float32)
            - jnp.dot(left_panel, top_panel, preferred_element_type=jnp.float32)
        ).astype(jnp.bfloat16)
    partial_value = jnp.dot(
        base_matrix, solution.reshape(cols_blk * blk_width), preferred_element_type=jnp.float32
    )
    totals = lax.psum(partial_value, "pcol")
    residual = right_side.reshape(rows_blk * blk_width) - totals
    res_blocks = residual.reshape(rows_blk, blk_width)
    slot_count = diagonal_block_inverses.shape[0]
    inverses = diagonal_block_inverses.reshape(slot_count, blk_width, blk_width)
    solve_count = slot_count * row_processors
    col_blocks = base_matrix.reshape(rows_blk * blk_width, cols_blk, blk_width)

    def carry_forward(blk_id, state):
        accum, solved = state
        owner_row = blk_id % row_processors
        slot_id = blk_id // row_processors
        pending = lax.dynamic_slice_in_dim(accum, slot_id * blk_width, blk_width, 0)
        res_block = lax.dynamic_slice_in_dim(res_blocks, slot_id, 1, 0)[0]
        inv_block = inverses[0].astype(jnp.float32)
        row_total = lax.psum(pending, "pcol")
        local_value = jnp.dot(inv_block, res_block - row_total, precision=lax.Precision.HIGHEST)
        new_value = broadcast(local_value, "prow", owner_row)
        rounded = new_value.astype(jnp.bfloat16)
        has_col = col_index == blk_id % col_devs
        col_piece = col_blocks[:, 0, :]
        product = jnp.dot(col_piece, rounded, preferred_element_type=jnp.float32)
        accum = accum + jnp.where(has_col, product, jnp.zeros_like(product))
        solved = lax.dynamic_update_slice_in_dim(solved, new_value[None], blk_id, 0)
        return (accum, solved)

    start = (
        jnp.zeros((rows_blk * blk_width,), jnp.float32),
        jnp.zeros((solve_count, blk_width), jnp.float32),
    )
    precond = lax.fori_loop(0, solve_count, carry_forward, start)[1]
    return (current.reshape(matrix.shape), residual.reshape(right_side.shape), precond)


def solution(mesh):
    return jax.shard_map(
        shards,
        mesh=mesh,
        in_specs=(
            P(None, "prow", None, None, "pcol", None),
            P(),
            P(),
            P(None, "pcol", None),
            P(None, "prow", None),
            P(None, "prow", None, None),
        ),
        out_specs=(P(None, "prow", None, None, "pcol", None), P(None, "prow", None), P()),
        check_vma=False,
    )
```

profile of v0, /device:TPU:135, one launch (start us, length us, event | category | flops | bytes accessed | tf_op | source)
XLA Modules:
  0.0 939.6 jit_solution(12790687416914332410)
XLA Ops:
  10.0 2.9 fusion.3
  13.6 59.0 %psum.69 = f32[2048]{0:T(1024)S(1)} all-reduce(f32[2048]{0:T(1024)S(1)} %bitcast.79), channel_id=1, replica_groups=mesh['prow'=8,'pcol'=32] {'pcol'}, use_global_device_ids=true, to_apply=%region_4.5 | all-reduce | flops 2048 | bytes 16384 | tf_op jit(solution)/shard_map/psum | solution.py:45
  72.7 3.7 all-reduce.7.cloned.1.call-done
  76.3 152.5 %all-reduce.5.cloned.1.call-done = bf16[2048,512]{0,1:T(8,128)(2,1)} async-done(((bf16[2048,512]{0,1:T(8,128)(2,1)}), bf16[2048,512]{0,1:T(8,128)(2,1)}) %all-reduce.5.cloned.1.call-update) | async-done | bytes 2097168 | tf_op jit(solution)/shard_map/psum | solution.py:11
  228.8 3.0 subtract_convert_fusion.1
  234.5 4.3 fusion.4
  239.8 688.2 %while.19 = (s32[]{:T(128)}, f32[2048]{0:T(1024)S(1)}, f32[8,512]{1,0:T(8,128)}, s32[]{:T(128)}, f32[4,512]{1,0:T(4,128)S(1)}, /*index=5*/bf16[1,1,512,512]{3,2,...) while((s32[]{:T(128)}, f32[2048]{0:T(1024)S(1)}, ...), condition=%wide.region_8.9_spmd.clone, body=%wide.region_5.8_spmd.clone.sunk | while | flops 5253665 | bytes 2712061 | solution.py:75
  239.9 58.1 %psum.74 = f32[512]{0:T(512)S(1)} all-reduce(f32[512]{0:T(512)S(1)} %dynamic_slice.28), channel_id=1, replica_groups=mesh['prow'=8,'pcol'=32] {'pcol'}, use_global_device_ids=true, to_apply=%region_6.6 | all-reduce | flops 512 | bytes 4096 | tf_op jit(solution)/shard_map/while/body/eval_jaxpr/psum | solution.py:60
  298.5 28.9 %psum.75 = f32[512]{0:T(512)S(1)} all-reduce(f32[512]{0:T(512)S(1)} %broadcast_select_fusion.5), channel_id=1, replica_groups=mesh['prow'=8,'pcol'=32] {'prow'}, use_global_device_ids=true, to_apply=%region_7.7 | all-reduce | flops 512 | bytes 4096 | tf_op jit(solution)/shard_map/while/body/eval_jaxpr/psum | solution.py:11
  329.5 55.9 %psum.74 = f32[512]{0:T(512)S(1)} all-reduce(f32[512]{0:T(512)S(1)} %dynamic_slice.28), channel_id=1, replica_groups=mesh['prow'=8,'pcol'=32] {'pcol'}, use_global_device_ids=true, to_apply=%region_6.6 | all-reduce | flops 512 | bytes 4096 | tf_op jit(solution)/shard_map/while/body/eval_jaxpr/psum | solution.py:60
  385.9 26.2 %psum.75 = f32[512]{0:T(512)S(1)} all-reduce(f32[512]{0:T(512)S(1)} %broadcast_select_fusion.5), channel_id=1, replica_groups=mesh['prow'=8,'pcol'=32] {'prow'}, use_global_device_ids=true, to_apply=%region_7.7 | all-reduce | flops 512 | bytes 4096 | tf_op jit(solution)/shard_map/while/body/eval_jaxpr/psum | solution.py:11
  414.2 57.9 %psum.74 = f32[512]{0:T(512)S(1)} all-reduce(f32[512]{0:T(512)S(1)} %dynamic_slice.28), channel_id=1, replica_groups=mesh['prow'=8,'pcol'=32] {'pcol'}, use_global_device_ids=true, to_apply=%region_6.6 | all-reduce | flops 512 | bytes 4096 | tf_op jit(solution)/shard_map/while/body/eval_jaxpr/psum | solution.py:60
  472.6 26.2 %psum.75 = f32[512]{0:T(512)S(1)} all-reduce(f32[512]{0:T(512)S(1)} %broadcast_select_fusion.5), channel_id=1, replica_groups=mesh['prow'=8,'pcol'=32] {'prow'}, use_global_device_ids=true, to_apply=%region_7.7 | all-reduce | flops 512 | bytes 4096 | tf_op jit(solution)/shard_map/while/body/eval_jaxpr/psum | solution.py:11
  500.9 55.7 %psum.74 = f32[512]{0:T(512)S(1)} all-reduce(f32[512]{0:T(512)S(1)} %dynamic_slice.28), channel_id=1, replica_groups=mesh['prow'=8,'pcol'=32] {'pcol'}, use_global_device_ids=true, to_apply=%region_6.6 | all-reduce | flops 512 | bytes 4096 | tf_op jit(solution)/shard_map/while/body/eval_jaxpr/psum | solution.py:60
  557.1 26.3 %psum.75 = f32[512]{0:T(512)S(1)} all-reduce(f32[512]{0:T(512)S(1)} %broadcast_select_fusion.5), channel_id=1, replica_groups=mesh['prow'=8,'pcol'=32] {'prow'}, use_global_device_ids=true, to_apply=%region_7.7 | all-reduce | flops 512 | bytes 4096 | tf_op jit(solution)/shard_map/while/body/eval_jaxpr/psum | solution.py:11
  585.5 57.4 %psum.74 = f32[512]{0:T(512)S(1)} all-reduce(f32[512]{0:T(512)S(1)} %dynamic_slice.28), channel_id=1, replica_groups=mesh['prow'=8,'pcol'=32] {'pcol'}, use_global_device_ids=true, to_apply=%region_6.6 | all-reduce | flops 512 | bytes 4096 | tf_op jit(solution)/shard_map/while/body/eval_jaxpr/psum | solution.py:60
  643.5 26.6 %psum.75 = f32[512]{0:T(512)S(1)} all-reduce(f32[512]{0:T(512)S(1)} %broadcast_select_fusion.5), channel_id=1, replica_groups=mesh['prow'=8,'pcol'=32] {'prow'}, use_global_device_ids=true, to_apply=%region_7.7 | all-reduce | flops 512 | bytes 4096 | tf_op jit(solution)/shard_map/while/body/eval_jaxpr/psum | solution.py:11
  672.2 55.7 %psum.74 = f32[512]{0:T(512)S(1)} all-reduce(f32[512]{0:T(512)S(1)} %dynamic_slice.28), channel_id=1, replica_groups=mesh['prow'=8,'pcol'=32] {'pcol'}, use_global_device_ids=true, to_apply=%region_6.6 | all-reduce | flops 512 | bytes 4096 | tf_op jit(solution)/shard_map/while/body/eval_jaxpr/psum | solution.py:60
  728.4 26.3 %psum.75 = f32[512]{0:T(512)S(1)} all-reduce(f32[512]{0:T(512)S(1)} %broadcast_select_fusion.5), channel_id=1, replica_groups=mesh['prow'=8,'pcol'=32] {'prow'}, use_global_device_ids=true, to_apply=%region_7.7 | all-reduce | flops 512 | bytes 4096 | tf_op jit(solution)/shard_map/while/body/eval_jaxpr/psum | solution.py:11
  756.8 57.4 %psum.74 = f32[512]{0:T(512)S(1)} all-reduce(f32[512]{0:T(512)S(1)} %dynamic_slice.28), channel_id=1, replica_groups=mesh['prow'=8,'pcol'=32] {'pcol'}, use_global_device_ids=true, to_apply=%region_6.6 | all-reduce | flops 512 | bytes 4096 | tf_op jit(solution)/shard_map/while/body/eval_jaxpr/psum | solution.py:60
  814.8 26.6 %psum.75 = f32[512]{0:T(512)S(1)} all-reduce(f32[512]{0:T(512)S(1)} %broadcast_select_fusion.5), channel_id=1, replica_groups=mesh['prow'=8,'pcol'=32] {'prow'}, use_global_device_ids=true, to_apply=%region_7.7 | all-reduce | flops 512 | bytes 4096 | tf_op jit(solution)/shard_map/while/body/eval_jaxpr/psum | solution.py:11
  843.5 55.7 %psum.74 = f32[512]{0:T(512)S(1)} all-reduce(f32[512]{0:T(512)S(1)} %dynamic_slice.28), channel_id=1, replica_groups=mesh['prow'=8,'pcol'=32] {'pcol'}, use_global_device_ids=true, to_apply=%region_6.6 | all-reduce | flops 512 | bytes 4096 | tf_op jit(solution)/shard_map/while/body/eval_jaxpr/psum | solution.py:60
  899.7 26.3 %psum.75 = f32[512]{0:T(512)S(1)} all-reduce(f32[512]{0:T(512)S(1)} %broadcast_select_fusion.5), channel_id=1, replica_groups=mesh['prow'=8,'pcol'=32] {'prow'}, use_global_device_ids=true, to_apply=%region_7.7 | all-reduce | flops 512 | bytes 4096 | tf_op jit(solution)/shard_map/while/body/eval_jaxpr/psum | solution.py:11
  928.1 5.0 subtract_convert_fusion
  (122 shorter events, 28.0 us)
Async XLA Ops:
  7.2 5.8 copy-start
  7.2 2.8 copy-start.1
  7.2 2.8 copy-start.6
  7.2 69.1 %all-reduce.7.cloned.1.call-start = ((), (), s32[]{:S(2)}) async-start(), calls=%async_computation.1 | async-start | bytes 1048576 | tf_op jit(solution)/shard_map/psum | solution.py:11
  9.9 218.9 %all-reduce.5.cloned.1.call-start = ((), (), s32[]{:S(2)}) async-start(), calls=%async_computation | async-start | bytes 4194304 | tf_op jit(solution)/shard_map/psum | solution.py:11
  12.8 59.8 %copy-start.4 = (f32[4,1,512]{2,1,0:T(1,128)S(1)}, f32[4,1,512]{2,1,0:T(1,128)}, u32[]{:S(2)}) copy-start(f32[4,1,512]{2,1,0:T(1,128)} %param.12) | copy-start | bytes 24580
  12.9 915.2 %all-reduce.11.cloned.1.call-start = ((), (), s32[]{:S(2)}) async-start(), calls=%async_computation.3 | async-start | bytes 1048576 | tf_op jit(solution)/shard_map/psum | solution.py:11
  72.6 159.2 %copy-start.3 = (f32[2048]{0:T(1024)}, f32[2048]{0:T(1024)S(1)}, u32[]{:S(2)}) copy-start(f32[2048]{0:T(1024)S(1)} %sub.28) | copy-start | bytes 24580
  72.6 160.5 %copy-start.5 = (bf16[2,512,512]{2,1,0:T(8,128)(2,1)S(1)}, bf16[2,512,512]{2,1,0:T(8,128)(2,1)}, u32[]{:S(2)}) copy-start(bf16[2,512,512]{2,1,0:T(8,128)(2,1)} %param.10) | copy-start | bytes 3145732
  231.8 1.3 copy-start.7
  234.4 693.6 %all-reduce.9.cloned.1.call-start = ((), (), s32[]{:S(2)}) async-start(), calls=%async_computation.2 | async-start | bytes 4194304 | tf_op jit(solution)/shard_map/psum | solution.py:11
  238.8 1.0 copy-start.2
Sparse Core Ops, SparseCore 0:
  10.4 65.9 all-reduce.6
  80.8 147.9 all-reduce.4
  234.5 68.5 all-reduce.10
  306.9 147.5 all-reduce.8
where the time goes:
time: 949 us; the launch traced here: 940 us
  blocking collectives  726 us (77%)
  waiting for transfers between devices  156 us (16%)
  matrix products  28.7 us (3%)
  local copies, waits for them, and re-layouts  13.9 us (1%)
  between operations  13.9 us (1%)
    psum x8, blocking collectives, carry_forward(): row_total = lax.psum(pending, 'pcol')  454 us
    psum x8, blocking collectives, broadcast(): return lax.psum(kept, axis)  214 us
    psum x4, waiting for transfers between devices, broadcast(): return lax.psum(kept, axis)  156 us
    psum x1, blocking collectives, shards(): totals = lax.psum(partial_value, 'pcol')  59 us
  transfers between devices with their start and end apart: 4, of which 2 were waited for; matrix products, arithmetic and copies ran while one was open for 3% of the time, Pallas kernels for 0%

commit v1 on v0

v1 whole, which is shorter than its diff:
```python
import jax
import jax.numpy as jnp
from jax import lax
from jax.experimental import pallas as pl
from jax.experimental.pallas import tpu as pltpu
from jax.sharding import PartitionSpec as P

MESH = pl.DeviceIdType.MESH
B = 512
CH = 64
NCD = B // CH
NCC = 64 // CH
NC = NCD + NCC
NPOS = 4
LAG_NUM, LAG_DEN = 3, 2
MAXD = 7
DIRS = ((1, 0), (-1, 0), (0, 1), (0, -1))
TREES = (
    (1, 29, 33, 48, 48, 39, 48, 96, 64, 55, 65, 88, 80, 71, 81, 96, 96, 83, 97, 112, 80, 66, 81, 96, 64, 59, 73, 84, 48, 43, 48, 96),
    (4, 80, 72, 48, 22, 72, 56, 42, 39, 56, 96, 48, 55, 64, 92, 70, 69, 84, 100, 84, 84, 100, 112, 100, 100, 112, 96, 112, 112, 96, 91, 96),
    (8, 80, 68, 48, 112, 96, 87, 96, 104, 112, 96, 112, 88, 104, 112, 104, 74, 88, 104, 90, 59, 73, 84, 64, 43, 52, 96, 48, 26, 68, 52, 38),
    (2, 48, 34, 30, 49, 64, 80, 37, 64, 80, 78, 55, 80, 96, 82, 65, 96, 112, 98, 81, 80, 96, 90, 75, 64, 80, 70, 59, 49, 64, 80, 41),
)
ROOT_DIR = (0, 2, 3, 1)
f32, bf16 = jnp.float32, jnp.bfloat16


def lag(depth):
    return depth * LAG_NUM // LAG_DEN


def dot(a, b):
    return jnp.dot(a, b, preferred_element_type=f32)


def dot_t(a, b):
    return lax.dot_general(a, b, (((1,), (1,)), ((), ())), preferred_element_type=f32)


def row_of(c):
    return jnp.concatenate([c[m : m + 1, :] for m in range(4)], axis=1)


def kernel(
    a_hbm, u_hbm, l_hbm, sol_ref, rhs_ref, inv_hbm,
    out_hbm, res_ref, pre_ref,
    a_v, strm, u_v, l_v, inv_v, chb, xb, comf, w_v, v_f, ry, rz, xs, acc, out_v,
    s_loc, s_out, s_send, s_recv, s_xsend, s_prim, s_oth, s_comsend, s_comx,
    s_blks, s_blkr, s_rys, s_ryr, s_rzs, s_rzr, s_xss, s_xsr, s_fs, s_fz, s_fy, s_cs, s_cr,
):
    p = lax.axis_index("prow")
    q = lax.axis_index("pcol")
    core = p % 2
    y, z = q % 4, q // 4
    is_q = q == 0

    def at(dy, dz):
        return ((z + dz + 8) % 8) * 4 + (y + dy + 4) % 4

    def rcopy(src, dst, ss, rs, dev):
        return pltpu.make_async_remote_copy(
            src_ref=src, dst_ref=dst, send_sem=ss, recv_sem=rs, device_id=dev, device_id_type=MESH
        )

    ld_a = pltpu.make_async_copy(a_hbm, a_v, s_loc.at[0])
    ld_u = pltpu.make_async_copy(u_hbm, u_v, s_loc.at[1])
    ld_l = pltpu.make_async_copy(l_hbm, l_v, s_loc.at[2])
    ld_i = pltpu.make_async_copy(inv_hbm, inv_v, s_loc.at[3])
    ld_a.start()
    for r in range(2):
        pl.when(q == r)(lambda r=r: pltpu.make_async_copy(a_hbm, strm.at[r, pl.ds(0, 4 * B)], s_loc.at[4]).start())
    src_com = (p + q) == 1

    def com_own():
        return pltpu.make_async_copy(
            a_hbm.at[pl.ds(pl.multiple_of(256 * core, 256), 256)], strm.at[q, pl.ds(4 * B, 256)], s_loc.at[5]
        )

    pl.when(src_com)(lambda: com_own().start())

    def xb_own():
        return pltpu.make_async_copy(a_hbm.at[pl.ds(0, B)], xb.at[core], s_loc.at[6])

    pl.when(p < 2)(lambda: xb_own().start())
    ld_u.start()
    ld_l.start()
    ld_i.start()

    bar = pltpu.get_barrier_semaphore()
    zm = [at(0, o) for o in range(1, 8)]
    ym = [at(o, 0) for o in range(1, 4)]
    pm = [(p + o) % 8 for o in range(1, 8)]
    for o in (3, 4, 2, 5, 1, 6, 0):
        pl.semaphore_signal(bar, inc=1, device_id=(p, zm[o]), device_id_type=MESH)
    for d in pm:
        pl.semaphore_signal(bar, inc=1, device_id=(d, q), device_id_type=MESH)
    for d in ym:
        pl.semaphore_signal(bar, inc=1, device_id=(p, d), device_id_type=MESH)

    @pl.when((q == 5) | (q == 6))
    def _():
        pl.semaphore_signal(bar, inc=1, device_id=(p, 0), device_id_type=MESH)

    @pl.when(is_q)
    def _():
        for d in (5, 6):
            pl.semaphore_signal(bar, inc=1, device_id=(p, d), device_id_type=MESH)

    ld_a.wait()
    sol8 = jnp.broadcast_to(sol_ref[...], (16, B))
    for i in range(4):
        part = dot_t(sol8, a_v[i * B : (i + 1) * B, :])
        for m in range(4):
            ry[y, 4 * i + m : 4 * i + m + 1, :] = part[0:1, 128 * m : 128 * (m + 1)]
    info = []
    for r in range(2):
        rel = z * 4 + (y + 4 - r) % 4
        word = jnp.int32(0)
        for k in range(32):
            packed = sum(TREES[t][k] << (7 * t) for t in range(4))
            word = jnp.where(rel == k, jnp.int32(packed), word)
        for t in range(4):
            v = (word // (128**t)) % 128
            dep, mask = v // 16, v % 16
            info.append((r, t, dep * LAG_NUM // LAG_DEN, [(mask // (1 << d)) % 2 for d in range(4)]))
    nbr = [at(dy, dz) for dy, dz in DIRS]
    for r in range(2):
        pl.when(q == r)(lambda r=r: pltpu.make_async_copy(a_hbm, strm.at[r, pl.ds(0, 4 * B)], s_loc.at[4]).wait())
    pl.semaphore_wait(bar, 17 + jnp.where(is_q, 2, jnp.where((q == 5) | (q == 6), 1, 0)))

    def rows(t, n):
        off = jnp.where(
            n < NPOS,
            B * t + CH * n,
            jnp.where(n < NPOS + NCC, 4 * B + 64 * t + CH * (n - NPOS), B * t + CH * (n - NCC)),
        )
        return pl.ds(pl.multiple_of(off, CH), CH)

    def hop(r, t, n, d):
        part = strm.at[r, rows(t, n)]
        return rcopy(part, part, s_send.at[r, t, d], s_recv.at[r, t, n], (p, nbr[d]))

    def inject(lo, hi):
        for r in range(2):

            @pl.when(q == r)
            def _():
                def one(n, c):
                    for t in range(4):
                        hop(r, t, n, ROOT_DIR[t]).start()
                    return c

                lax.fori_loop(lo, hi, one, 0)

    def ry_copy(o):
        return rcopy(ry.at[y], ry.at[y], s_rys.at[o], s_ryr.at[y], (p, ym[o]))

    for o in range(3):
        ry_copy(o).start()
    inject(0, NPOS)

    def com_copy(o):
        half = (pm[o]) % 2
        return rcopy(
            a_v.at[pl.ds(pl.multiple_of(256 * half, 256), 256)], strm.at[q, pl.ds(4 * B, 256)],
            s_comsend.at[o], s_comx, (pm[o], q),
        )

    @pl.when(src_com)
    def _():
        for o in (0, 1, 6, 5, 2, 4, 3):
            com_copy(o).start()
        com_own().wait()

    def blk_copy(j):
        return rcopy(a_v.at[pl.ds(0, B)], chb.at[j - 1], s_blks, s_blkr.at[j - 1], (p, 0))

    for j in range(1, 7):
        pl.when((q == j) & (p > j))(lambda j=j: blk_copy(j).start())

    def xb_copy(o):
        return rcopy(xb.at[core], xb.at[core], s_xsend.at[o], s_prim, (2 * (o + 1) + core, q))

    def xb_pair():
        return rcopy(xb.at[core], xb.at[core], s_xsend.at[3], s_oth, (p + 1 - 2 * core, q))

    @pl.when(p < 2)
    def _():
        xb_own().wait()
        xb_pair().start()
        for o in (0, 2, 1):
            xb_copy(o).start()

    def ticks(lo, hi):
        def one(k, c):
            for r, t, lg, kids in info:
                n = k - lg

                @pl.when((n >= 0) & (n < NC) & (q != r))
                def _():
                    hop(r, t, n, 0).wait_recv()
                    for d in range(4):
                        pl.when(kids[d] == 1)(lambda d=d: hop(r, t, n, d).start())

            return c

        lax.fori_loop(lo, hi, one, 0)

    def rz_copy(o):
        return rcopy(rz.at[z], rz.at[z], s_rzs.at[o], s_rzr.at[z], (p, zm[o]))

    def ev_y():
        for o in range(1, 4):
            src = (y + o) % 4
            rcopy(ry.at[src], ry.at[src], s_rys.at[0], s_ryr.at[src], (p, ym[0])).wait_recv()
        rz[z] = ((ry[0] + ry[1]) + (ry[2] + ry[3]))
        for o in (3, 4, 2, 5, 1, 6, 0):
            rz_copy(o).start()

    def ev_z():
        for o in range(1, 8):
            src = (z + o) % 8
            rcopy(rz.at[src], rz.at[src], s_rzs.at[0], s_rzr.at[src], (p, zm[0])).wait_recv()
        tot = rz[0]
        for k in range(1, 8):
            tot = tot + rz[k]
        for i in range(4):
            res_ref[i : i + 1, :] = rhs_ref[i : i + 1, :] - row_of(tot[4 * i : 4 * i + 4, :])

        @pl.when(is_q)
        def _():
            acc[0:1, :] = res_ref[0:1, :]

    def x_copy(j, o):
        return rcopy(xs.at[j], xs.at[j], s_xss.at[o], s_xsr.at[j], ((j + o) % 8, 0))

    def x_recv(j):
        rcopy(xs.at[j], xs.at[j], s_xss.at[0], s_xsr.at[j], ((p + 1) % 8, 0)).wait_recv()

    def ev_c(j):
        @pl.when(is_q & (p > j))
        def _():
            blk = a_v.at[pl.ds(0, B)] if j == 0 else chb.at[j - 1]
            if j:
                rcopy(a_v.at[pl.ds(0, B)], chb.at[j - 1], s_blks, s_blkr.at[j - 1], ((p + 1) % 8, 0)).wait_recv()
            x_recv(j)
            row = row_of(xs[j, 0:4, :]).astype(bf16)
            acc[0:1, :] = acc[0:1, :] - dot_t(jnp.broadcast_to(row, (16, B)), blk[...])[0:1, :]

        @pl.when(is_q & (p == j))
        def _():
            if j == 0:
                pass
            s = acc[0:1, :]
            hi = s.astype(bf16).astype(f32)
            mid = (s - hi).astype(bf16).astype(f32)
            lo = (s - hi - mid).astype(bf16).astype(f32)
            k = lax.broadcasted_iota(jnp.int32, (16, B), 0)
            lhs = jnp.where(k == 0, hi, jnp.where(k == 1, mid, jnp.where(k == 2, lo, 0.0)))
            r3 = dot_t(lhs.astype(bf16), inv_v[...])
            x = (r3[0:1, :] + r3[1:2, :]) + r3[2:3, :]
            for m in range(4):
                xs[j, m : m + 1, :] = x[:, 128 * m : 128 * (m + 1)]
            xs[j, 4:8, :] = jnp.zeros((4, 128), f32)
            for o in (1, 2, 3, 4, 5, 6, 7):
                x_copy(j, o).start()

    def fz_copy(o):
        return rcopy(xs, xs, s_fs.at[o], s_fz, (p, zm[o]))

    def fy_copy(o):
        return rcopy(xs, xs, s_fs.at[7 + o], s_fy, (p, ym[o]))

    def ev_f0():
        @pl.when(is_q)
        def _():
            for j in range(8):
                pl.when(p < j)(lambda j=j: x_recv(j))
            for o in (3, 4, 2, 5, 1, 6, 0):
                fz_copy(o).start()
            for o in range(3):
                fy_copy(o).start()

    def ev_f1():
        @pl.when((y == 0) & (z != 0))
        def _():
            fz_copy(0).wait_recv()
            for o in range(3):
                fy_copy(o).start()

    def ev_f2():
        pl.when(y != 0)(lambda: fy_copy(0).wait_recv())
        for j in range(8):
            pre_ref[j : j + 1, :] = row_of(xs[j, 0:4, :])

    def tri(m, low):
        a = lax.broadcasted_iota(jnp.int32, (B, B), 0)
        b = lax.broadcasted_iota(jnp.int32, (B, B), 1)
        return jnp.where((a >= b) if low else (a <= b), m.astype(f32), 0.0).astype(bf16)

    def ev_v():
        ld_u.wait()
        ld_l.wait()
        for k in range(2):
            u_v[k] = tri(u_v[k], False)
            l_v[k] = tri(l_v[k], True)

    def ev_x():
        @pl.when(p >= 2)
        def _():
            rcopy(xb.at[core], xb.at[core], s_xsend.at[0], s_prim, (p, nbr[0])).wait_recv()
            xb_pair().start()

        rcopy(xb.at[1 - core], xb.at[1 - core], s_xsend.at[0], s_oth, (p, nbr[0])).wait_recv()
        v_f[...] = dot(u_v[0], dot(l_v[0], xb[0]).astype(bf16))

    def c_copy(r):
        mine = comf.at[r, pl.ds(pl.multiple_of(256 * core, 256), 256)]
        return rcopy(strm.at[r, pl.ds(4 * B, 256)], mine, s_cs.at[r], s_cr.at[r], (p + 1 - 2 * core, q))

    def ev_com():
        for r in range(2):
            c_copy(r).start()
            comf[r, pl.ds(pl.multiple_of(256 * core, 256), 256)] = strm[r, 4 * B : 4 * B + 256]

    def ev_w():
        for r in range(2):
            other = comf.at[r, pl.ds(pl.multiple_of(256 - 256 * core, 256), 256)]
            rcopy(other, other, s_cs.at[r], s_cr.at[r], (p + 1 - 2 * core, q)).wait_recv()
        v = v_f[...]
        d = (xb[1].astype(f32) - dot(comf[0], v.astype(bf16))).astype(bf16)
        w1 = dot(u_v[1], dot(l_v[1], d).astype(bf16)).astype(bf16)
        w_v[1] = w1
        v1 = dot(u_v[0], dot(l_v[0], comf[1]).astype(bf16)).astype(bf16)
        w_v[0] = (v - dot(v1, w1)).astype(bf16)

    last = NC - 1 + lag(MAXD) + 1
    com_tick = NPOS + NCC + lag(MAXD)
    events = [
        (0, ev_v), (1, ev_y), (2, ev_z),
        (NPOS, lambda: com_ready()),
    ]
    for j in range(8):
        events.append((min(2 + j, last), lambda j=j: ev_c(j)))
    events += [(9, ev_x), (10, ev_f0), (12, ev_f1), (com_tick, ev_com), (com_tick + 1, ev_w)]

    def com_ready():
        for r in range(2):
            pl.when((q == r) & jnp.logical_not(src_com))(lambda r=r: com_copy(0).wait_recv())
        inject(NPOS, NC)

    ld_i.wait()
    now = 0
    for when, ev in sorted(events, key=lambda e: e[0]):
        when = min(when, last)
        if when > now:
            ticks(now, when)
            now = when
        ev()
    if now < last:
        ticks(now, last)

    def step(s, c):
        i256 = pl.ds(pl.multiple_of(s * 256, 256), 256)
        prod = dot(strm[0, i256], w_v[0]) + dot(strm[1, i256], w_v[1])
        out_v[i256] = (a_v[i256].astype(f32) - prod).astype(bf16)
        pltpu.make_async_copy(out_v.at[i256], out_hbm.at[i256], s_out).start()
        return c

    lax.fori_loop(0, 8, step, 0)
    ev_f2()

    for r, t, lg, kids in info:
        for d in range(4):
            sent = strm.at[r, pl.ds(0, NC * CH)]
            pl.when(kids[d] == 1)(
                lambda r=r, t=t, d=d, sent=sent: rcopy(sent, sent, s_send.at[r, t, d], s_recv.at[r, t, 0], (p, nbr[d])).wait_send()
            )
    for o in range(3):
        ry_copy(o).wait_send()
    for o in range(7):
        rz_copy(o).wait_send()

    @pl.when(src_com)
    def _():
        for o in range(7):
            com_copy(o).wait_send()

    for j in range(1, 7):
        pl.when((q == j) & (p > j))(lambda j=j: blk_copy(j).wait_send())
    xb_pair().wait_send()

    @pl.when(p < 2)
    def _():
        for o in range(3):
            xb_copy(o).wait_send()

    for r in range(2):
        c_copy(r).wait_send()

    @pl.when(is_q)
    def _():
        for o in range(1, 8):
            x_copy(0, o).wait_send()
        for o in range(7):
            fz_copy(o).wait_send()

    @pl.when(y == 0)
    def _():
        for o in range(3):
            fy_copy(o).wait_send()

    pltpu.make_async_copy(out_v, out_hbm, s_out).wait()


def shards(matrix, upper_inv, lower_inv, solution, right_side, diagonal_block_inverses):
    dma, vm = pltpu.SemaphoreType.DMA, pltpu.VMEM
    hbm = pl.BlockSpec(memory_space=pl.ANY)
    vmem = pl.BlockSpec(memory_space=pltpu.VMEM)
    updated, residual, precond = pl.pallas_call(
        kernel,
        out_shape=(
            jax.ShapeDtypeStruct((4 * B, B), bf16),
            jax.ShapeDtypeStruct((4, B), f32),
            jax.ShapeDtypeStruct((8, B), f32),
        ),
        in_specs=[hbm, hbm, hbm, vmem, vmem, hbm],
        out_specs=(hbm, vmem, vmem),
        scratch_shapes=[
            vm((4 * B, B), bf16), vm((2, 4 * B + 256, B), bf16), vm((2, B, B), bf16), vm((2, B, B), bf16),
            vm((B, B), bf16), vm((6, B, B), bf16), vm((2, B, B), bf16), vm((2, B, B), bf16), vm((2, B, B), bf16),
            vm((B, B), f32), vm((4, 16, 128), f32), vm((8, 16, 128), f32), vm((8, 8, 128), f32), vm((8, B), f32),
            vm((4 * B, B), bf16),
            dma((7,)), dma, dma((2, 4, 4)), dma((2, 4, NC)), dma((4,)), dma, dma, dma((7,)), dma,
            dma, dma((6,)), dma((3,)), dma((4,)), dma((7,)), dma((8,)), dma((8,)), dma((8,)), dma((10,)), dma, dma,
            dma((2,)), dma((2,)),
        ],
        compiler_params=pltpu.CompilerParams(collective_id=0, has_side_effects=True, vmem_limit_bytes=56 << 20),
        cost_estimate=pl.CostEstimate(flops=8 << 30, bytes_accessed=8 << 20, transcendentals=0),
    )(
        matrix.reshape(4 * B, B),
        upper_inv,
        lower_inv,
        solution.reshape(1, B),
        right_side.reshape(4, B),
        diagonal_block_inverses.reshape(B, B),
    )
    return updated.reshape(matrix.shape), residual.reshape(right_side.shape), precond


def solution(mesh):
    return jax.shard_map(
        shards,
        mesh=mesh,
        in_specs=(
            P(None, "prow", None, None, "pcol", None),
            P(),
            P(),
            P(None, "pcol", None),
            P(None, "prow", None),
            P(None, "prow", None, None),
        ),
        out_specs=(P(None, "prow", None, None, "pcol", None), P(None, "prow", None), P()),
        check_vma=False,
    )
```

time: 949 us -> 107 us (0.11)
  the two profiles are of different devices: /device:TPU:135 before, /device:TPU:44 now
where the time goes in v1:
time: 107 us
  Pallas kernels  99.9 us (93%)
  local copies, waits for them, and re-layouts  6.27 us (6%)
    pallas_call x1, Pallas kernels, shards(): pl.pallas_call(kernel, out_shape=(jax.ShapeDtypeStruct((4 * B, B), bf16),...  99.9 us
    unnamed x6, local copies, waits for them, and re-layouts  6.27 us

profile of v1, /device:TPU:44, one launch (start us, length us, event | category | flops | bytes accessed | tf_op | source)
XLA Modules:
  0.0 106.8 jit_solution(8359731103207092438)
XLA Ops:
  0.6 1.3 %copy.13 = f32[4,1,512]{2,0,1:T(4,128)} copy(f32[4,1,512]{2,1,0:T(1,128)} %param.10) | data formatting | bytes 16384
  1.9 99.9 %shard_map.85 = (bf16[2048,512]{1,0:T(8,128)(2,1)}, f32[4,512]{1,0:T(4,128)}, f32[8,512]{1,0:T(8,128)}) custom-call(bf16[2048,512]{1,0:T(8,128)(2,1)} %bitcast.13, bf16[2,512,512]{2,1,0:T(8,128)(2,1)} %u_hbm.1, bf16[2,512,512]{2,1,0:T(8,128)(2,1)} %l_hbm.1, bf16[1,512]{1,0:T(2,128)(2,1)} %bitcast.15, f32[4,512]{1,0:T(4,128)} %bitcast.12, ...), custom_call_target="tpu_custom_call" | custom-call | flops 8589934592 | bytes 8388608 | tf_op jit(solution)/shard_map/pallas_call | solution.py:420
  101.8 1.3 %copy.10 = f32[4,1,512]{2,1,0:T(1,128)} copy(f32[4,1,512]{2,0,1:T(4,128)} %bitcast.11) | data formatting | bytes 16384
  103.1 0.0 copy-start
  103.1 3.1 %copy.16 = bf16[4,1,512,1,1,512]{5,2,4,3,1,0:T(8,128)(2,1)} copy(bf16[4,1,512,1,1,512]{5,2,4,3,1,0:T(8,128)(2,1)} %bitcast.10) | data formatting | bytes 4194304
  106.2 0.0 copy-done
  106.2 0.6 copy.17
Async XLA Ops:
  103.1 3.1 %copy-start = (f32[8,512]{1,0:T(8,128)S(1)}, f32[8,512]{1,0:T(8,128)}, u32[]{:S(2)}) copy-start(f32[8,512]{1,0:T(8,128)} %get-tuple-element.17) | copy-start | bytes 49156

commit v2 on v1

--- a/solution.py
+++ b/solution.py
@@ -8,25 +8,31 @@
 MESH = pl.DeviceIdType.MESH
 B = 512
 CH = 64
-NCD = B // CH
-NCC = 64 // CH
-NC = NCD + NCC
-NPOS = 4
-LAG_NUM, LAG_DEN = 3, 2
-MAXD = 7
+CR = 16
+NPOS = 3
+NC = B // CH + 1
 DIRS = ((1, 0), (-1, 0), (0, 1), (0, -1))
-TREES = (
-    (1, 29, 33, 48, 48, 39, 48, 96, 64, 55, 65, 88, 80, 71, 81, 96, 96, 83, 97, 112, 80, 66, 81, 96, 64, 59, 73, 84, 48, 43, 48, 96),
-    (4, 80, 72, 48, 22, 72, 56, 42, 39, 56, 96, 48, 55, 64, 92, 70, 69, 84, 100, 84, 84, 100, 112, 100, 100, 112, 96, 112, 112, 96, 91, 96),
-    (8, 80, 68, 48, 112, 96, 87, 96, 104, 112, 96, 112, 88, 104, 112, 104, 74, 88, 104, 90, 59, 73, 84, 64, 43, 52, 96, 48, 26, 68, 52, 38),
-    (2, 48, 34, 30, 49, 64, 80, 37, 64, 80, 78, 55, 80, 96, 82, 65, 96, 112, 98, 81, 80, 96, 90, 75, 64, 80, 70, 59, 49, 64, 80, 41),
+TABLE = (
+    (
+        (2049, 221261, 184641, 147824, 27936, 217255, 151904, 95728, 53056, 69879, 246113, 115112, 85856, 229655, 145761, 101824, 109488, 141619, 190849, 141760, 125360, 198994, 254353, 158160, 182576, 229643, 205177, 254356, 237984, 229563, 194432, 254432),
+        (1032, 237952, 66900, 64752, 164736, 254416, 205191, 117664, 188728, 156096, 138720, 126928, 196872, 229736, 181696, 131864, 237786, 246056, 173400, 140042, 213163, 229657, 152932, 120768, 147563, 155828, 126448, 112544, 82506, 106788, 221364, 70310),
+    ),
+    (
+        (205006, 2050, 147856, 201010, 151799, 11104, 62448, 152016, 78087, 44896, 156056, 196962, 254247, 69424, 93040, 129330, 158019, 85376, 133552, 190834, 207185, 141808, 158160, 229730, 213259, 158016, 197012, 229722, 221435, 172368, 246192, 210768),
+        (123360, 520, 23360, 74660, 205248, 124352, 60896, 229815, 147952, 139528, 85984, 121792, 246120, 155880, 99624, 140224, 205128, 213177, 140553, 181048, 254218, 180395, 128848, 168772, 180388, 163947, 71552, 117728, 164068, 82969, 62613, 196916),
+    ),
 )
-ROOT_DIR = (0, 2, 3, 1)
+ROOT_DIR = ((0, 2, 3, 1), (1, 2, 3, 0))
+LAG_MAX = 31
+EY = 2
+EZ = 7
+EX = 15
+EC = (8, 10, 13, 16, 19, 21, 24, 27)
+EF0 = 30
+EF1 = 33
+EP = 99
+EW = 99
 f32, bf16 = jnp.float32, jnp.bfloat16
-
-
-def lag(depth):
-    return depth * LAG_NUM // LAG_DEN
 
 
 def dot(a, b):
@@ -44,9 +50,9 @@
 def kernel(
     a_hbm, u_hbm, l_hbm, sol_ref, rhs_ref, inv_hbm,
     out_hbm, res_ref, pre_ref,
-    a_v, strm, u_v, l_v, inv_v, chb, xb, comf, w_v, v_f, ry, rz, xs, acc, out_v,
+    a_v, strm, u_v, l_v, inv_v, chb, xb, comf, w_v, v_f, ry, rz, xs, pk, acc, out_v,
     s_loc, s_out, s_send, s_recv, s_xsend, s_prim, s_oth, s_comsend, s_comx,
-    s_blks, s_blkr, s_rys, s_ryr, s_rzs, s_rzr, s_xss, s_xsr, s_fs, s_fz, s_fy, s_cs, s_cr,
+    s_blks, s_blkr, s_rys, s_ryr, s_rzs, s_rzr, s_xss, s_xsr, s_fs, s_fz, s_fy, s_cs, s_cr, s_gs, s_gr,
 ):
     p = lax.axis_index("prow")
     q = lax.axis_index("pcol")
@@ -71,9 +77,12 @@
         pl.when(q == r)(lambda r=r: pltpu.make_async_copy(a_hbm, strm.at[r, pl.ds(0, 4 * B)], s_loc.at[4]).start())
     src_com = (p + q) == 1
 
+    def piece(d):
+        return pl.ds(pl.multiple_of(64 * (4 * (d % 2) + d // 2), 64), 64)
+
     def com_own():
         return pltpu.make_async_copy(
-            a_hbm.at[pl.ds(pl.multiple_of(256 * core, 256), 256)], strm.at[q, pl.ds(4 * B, 256)], s_loc.at[5]
+            a_hbm.at[piece(p)], strm.at[q, pl.ds(4 * B, 64)], s_loc.at[5]
         )
 
     pl.when(src_com)(lambda: com_own().start())
@@ -85,6 +94,18 @@
     ld_u.start()
     ld_l.start()
     ld_i.start()
+
+    def tri(m, low):
+        a = lax.broadcasted_iota(jnp.int32, (B, B), 0)
+        b = lax.broadcasted_iota(jnp.int32, (B, B), 1)
+        return jnp.where((a >= b) if low else (a <= b), m.astype(f32), 0.0).astype(bf16)
+
+    def ev_v():
+        ld_u.wait()
+        ld_l.wait()
+        for k in range(2):
+            u_v[k] = tri(u_v[k], False)
+            l_v[k] = tri(l_v[k], True)
 
     bar = pltpu.get_barrier_semaphore()
     zm = [at(0, o) for o in range(1, 8)]
@@ -114,31 +135,28 @@
             ry[y, 4 * i + m : 4 * i + m + 1, :] = part[0:1, 128 * m : 128 * (m + 1)]
     info = []
     for r in range(2):
-        rel = z * 4 + (y + 4 - r) % 4
-        word = jnp.int32(0)
-        for k in range(32):
-            packed = sum(TREES[t][k] << (7 * t) for t in range(4))
-            word = jnp.where(rel == k, jnp.int32(packed), word)
-        for t in range(4):
-            v = (word // (128**t)) % 128
-            dep, mask = v // 16, v % 16
-            info.append((r, t, dep * LAG_NUM // LAG_DEN, [(mask // (1 << d)) % 2 for d in range(4)]))
+        for h in range(2):
+            word = jnp.int32(0)
+            for k in range(32):
+                word = jnp.where(q == k, jnp.int32(TABLE[r][h][k]), word)
+            for t in range(2):
+                v = (word // (512**t)) % 512
+                mask = v % 16
+                info.append((r, 2 * h + t, v // 16, [(mask // (1 << d)) % 2 for d in range(4)]))
     nbr = [at(dy, dz) for dy, dz in DIRS]
     for r in range(2):
         pl.when(q == r)(lambda r=r: pltpu.make_async_copy(a_hbm, strm.at[r, pl.ds(0, 4 * B)], s_loc.at[4]).wait())
+    ev_v()
+    ld_i.wait()
     pl.semaphore_wait(bar, 17 + jnp.where(is_q, 2, jnp.where((q == 5) | (q == 6), 1, 0)))
 
-    def rows(t, n):
-        off = jnp.where(
-            n < NPOS,
-            B * t + CH * n,
-            jnp.where(n < NPOS + NCC, 4 * B + 64 * t + CH * (n - NPOS), B * t + CH * (n - NCC)),
-        )
-        return pl.ds(pl.multiple_of(off, CH), CH)
-
     def hop(r, t, n, d):
-        part = strm.at[r, rows(t, n)]
+        part = strm.at[r, pl.ds(pl.multiple_of(B * t + CH * jnp.where(n > NPOS, n - 1, n), CH), CH)]
         return rcopy(part, part, s_send.at[r, t, d], s_recv.at[r, t, n], (p, nbr[d]))
+
+    def com_hop(r, t, d):
+        part = strm.at[r, pl.ds(4 * B + CR * t, CR)]
+        return rcopy(part, part, s_send.at[r, t, d], s_recv.at[r, t, NPOS], (p, nbr[d]))
 
     def inject(lo, hi):
         for r in range(2):
@@ -147,7 +165,7 @@
             def _():
                 def one(n, c):
                     for t in range(4):
-                        hop(r, t, n, ROOT_DIR[t]).start()
+                        hop(r, t, n, ROOT_DIR[r][t]).start()
                     return c
 
                 lax.fori_loop(lo, hi, one, 0)
@@ -160,10 +178,8 @@
     inject(0, NPOS)
 
     def com_copy(o):
-        half = (pm[o]) % 2
         return rcopy(
-            a_v.at[pl.ds(pl.multiple_of(256 * half, 256), 256)], strm.at[q, pl.ds(4 * B, 256)],
-            s_comsend.at[o], s_comx, (pm[o], q),
+            a_v.at[piece(pm[o])], strm.at[q, pl.ds(4 * B, 64)], s_comsend.at[o], s_comx, (pm[o], q)
         )
 
     @pl.when(src_com)
@@ -195,12 +211,19 @@
         def one(k, c):
             for r, t, lg, kids in info:
                 n = k - lg
-
-                @pl.when((n >= 0) & (n < NC) & (q != r))
+                other = q != r
+
+                @pl.when((n >= 0) & (n < NC) & (n != NPOS) & other)
                 def _():
                     hop(r, t, n, 0).wait_recv()
                     for d in range(4):
                         pl.when(kids[d] == 1)(lambda d=d: hop(r, t, n, d).start())
+
+                @pl.when((n == NPOS) & other)
+                def _():
+                    com_hop(r, t, 0).wait_recv()
+                    for d in range(4):
+                        pl.when(kids[d] == 1)(lambda d=d: com_hop(r, t, d).start())
 
             return c
 
@@ -225,11 +248,11 @@
         for k in range(1, 8):
             tot = tot + rz[k]
         for i in range(4):
-            res_ref[i : i + 1, :] = rhs_ref[i : i + 1, :] - row_of(tot[4 * i : 4 * i + 4, :])
+            res_ref[i] = rhs_ref[i] - row_of(tot[4 * i : 4 * i + 4, :])
 
         @pl.when(is_q)
         def _():
-            acc[0:1, :] = res_ref[0:1, :]
+            acc[0:1, :] = res_ref[0]
 
     def x_copy(j, o):
         return rcopy(xs.at[j], xs.at[j], s_xss.at[o], s_xsr.at[j], ((j + o) % 8, 0))
@@ -266,16 +289,18 @@
                 x_copy(j, o).start()
 
     def fz_copy(o):
-        return rcopy(xs, xs, s_fs.at[o], s_fz, (p, zm[o]))
+        return rcopy(pk, pk, s_fs.at[o], s_fz, (p, zm[o]))
 
     def fy_copy(o):
-        return rcopy(xs, xs, s_fs.at[7 + o], s_fy, (p, ym[o]))
+        return rcopy(pk, pk, s_fs.at[7 + o], s_fy, (p, ym[o]))
 
     def ev_f0():
         @pl.when(is_q)
         def _():
             for j in range(8):
                 pl.when(p < j)(lambda j=j: x_recv(j))
+            for j in range(8):
+                pk[4 * j : 4 * j + 4, :] = xs[j, 0:4, :]
             for o in (3, 4, 2, 5, 1, 6, 0):
                 fz_copy(o).start()
             for o in range(3):
@@ -291,19 +316,7 @@
     def ev_f2():
         pl.when(y != 0)(lambda: fy_copy(0).wait_recv())
         for j in range(8):
-            pre_ref[j : j + 1, :] = row_of(xs[j, 0:4, :])
-
-    def tri(m, low):
-        a = lax.broadcasted_iota(jnp.int32, (B, B), 0)
-        b = lax.broadcasted_iota(jnp.int32, (B, B), 1)
-        return jnp.where((a >= b) if low else (a <= b), m.astype(f32), 0.0).astype(bf16)
-
-    def ev_v():
-        ld_u.wait()
-        ld_l.wait()
-        for k in range(2):
-            u_v[k] = tri(u_v[k], False)
-            l_v[k] = tri(l_v[k], True)
+            pre_ref[j : j + 1, :] = row_of(pk[4 * j : 4 * j + 4, :])
 
     def ev_x():
         @pl.when(p >= 2)
@@ -314,14 +327,30 @@
         rcopy(xb.at[1 - core], xb.at[1 - core], s_xsend.at[0], s_oth, (p, nbr[0])).wait_recv()
         v_f[...] = dot(u_v[0], dot(l_v[0], xb[0]).astype(bf16))
 
+    half = pl.ds(pl.multiple_of(256 * core, 256), 256)
+
+    def g_copy(r, o):
+        return rcopy(
+            strm.at[r, pl.ds(4 * B, 64)], comf.at[r, piece(p)], s_gs.at[r, o], s_gr.at[r, p // 2], (pm[2 * o + 1], q)
+        )
+
     def c_copy(r):
-        mine = comf.at[r, pl.ds(pl.multiple_of(256 * core, 256), 256)]
-        return rcopy(strm.at[r, pl.ds(4 * B, 256)], mine, s_cs.at[r], s_cr.at[r], (p + 1 - 2 * core, q))
+        return rcopy(comf.at[r, half], comf.at[r, half], s_cs.at[r], s_cr.at[r], (p + 1 - 2 * core, q))
 
     def ev_com():
         for r in range(2):
+            for o in range(3):
+                g_copy(r, o).start()
+            comf[r, piece(p)] = strm[r, 4 * B : 4 * B + 64]
+
+    def ev_pair():
+        for r in range(2):
+            for o in range(3):
+                src = pm[2 * o + 1]
+                rcopy(
+                    strm.at[r, pl.ds(4 * B, 64)], comf.at[r, piece(src)], s_gs.at[r, o], s_gr.at[r, src // 2], (src, q)
+                ).wait_recv()
             c_copy(r).start()
-            comf[r, pl.ds(pl.multiple_of(256 * core, 256), 256)] = strm[r, 4 * B : 4 * B + 256]
 
     def ev_w():
         for r in range(2):
@@ -334,22 +363,18 @@
         v1 = dot(u_v[0], dot(l_v[0], comf[1]).astype(bf16)).astype(bf16)
         w_v[0] = (v - dot(v1, w1)).astype(bf16)
 
-    last = NC - 1 + lag(MAXD) + 1
-    com_tick = NPOS + NCC + lag(MAXD)
-    events = [
-        (0, ev_v), (1, ev_y), (2, ev_z),
-        (NPOS, lambda: com_ready()),
-    ]
-    for j in range(8):
-        events.append((min(2 + j, last), lambda j=j: ev_c(j)))
-    events += [(9, ev_x), (10, ev_f0), (12, ev_f1), (com_tick, ev_com), (com_tick + 1, ev_w)]
+    last = NC + LAG_MAX
+    events = [(0, lambda: com_ready()), (EY, ev_y), (EZ, ev_z), (EX, ev_x), (EF0, ev_f0), (EF1, ev_f1)]
+    events += [(EC[j], lambda j=j: ev_c(j)) for j in range(8)]
+    events += [(NPOS + 1 + LAG_MAX, ev_com), (EP, ev_pair), (EW, ev_w)]
 
     def com_ready():
         for r in range(2):
             pl.when((q == r) & jnp.logical_not(src_com))(lambda r=r: com_copy(0).wait_recv())
-        inject(NPOS, NC)
-
-    ld_i.wait()
+        for r in range(2):
+            pl.when(q == r)(lambda r=r: [com_hop(r, t, ROOT_DIR[r][t]).start() for t in range(4)] and None)
+        inject(NPOS + 1, NC)
+
     now = 0
     for when, ev in sorted(events, key=lambda e: e[0]):
         when = min(when, last)
@@ -372,7 +397,7 @@
 
     for r, t, lg, kids in info:
         for d in range(4):
-            sent = strm.at[r, pl.ds(0, NC * CH)]
+            sent = strm.at[r, pl.ds(0, B + CR)]
             pl.when(kids[d] == 1)(
                 lambda r=r, t=t, d=d, sent=sent: rcopy(sent, sent, s_send.at[r, t, d], s_recv.at[r, t, 0], (p, nbr[d])).wait_send()
             )
@@ -397,6 +422,8 @@
 
     for r in range(2):
         c_copy(r).wait_send()
+        for o in range(3):
+            g_copy(r, o).wait_send()
 
     @pl.when(is_q)
     def _():
@@ -421,19 +448,19 @@
         kernel,
         out_shape=(
             jax.ShapeDtypeStruct((4 * B, B), bf16),
-            jax.ShapeDtypeStruct((4, B), f32),
+            jax.ShapeDtypeStruct((4, 1, B), f32),
             jax.ShapeDtypeStruct((8, B), f32),
         ),
         in_specs=[hbm, hbm, hbm, vmem, vmem, hbm],
         out_specs=(hbm, vmem, vmem),
         scratch_shapes=[
-            vm((4 * B, B), bf16), vm((2, 4 * B + 256, B), bf16), vm((2, B, B), bf16), vm((2, B, B), bf16),
+            vm((4 * B, B), bf16), vm((2, 4 * B + 64, B), bf16), vm((2, B, B), bf16), vm((2, B, B), bf16),
             vm((B, B), bf16), vm((6, B, B), bf16), vm((2, B, B), bf16), vm((2, B, B), bf16), vm((2, B, B), bf16),
-            vm((B, B), f32), vm((4, 16, 128), f32), vm((8, 16, 128), f32), vm((8, 8, 128), f32), vm((8, B), f32),
+            vm((B, B), f32), vm((4, 16, 128), f32), vm((8, 16, 128), f32), vm((8, 8, 128), f32), vm((32, 128), f32), vm((8, B), f32),
             vm((4 * B, B), bf16),
             dma((7,)), dma, dma((2, 4, 4)), dma((2, 4, NC)), dma((4,)), dma, dma, dma((7,)), dma,
             dma, dma((6,)), dma((3,)), dma((4,)), dma((7,)), dma((8,)), dma((8,)), dma((8,)), dma((10,)), dma, dma,
-            dma((2,)), dma((2,)),
+            dma((2,)), dma((2,)), dma((2, 3)), dma((2, 4)),
         ],
         compiler_params=pltpu.CompilerParams(collective_id=0, has_side_effects=True, vmem_limit_bytes=56 << 20),
         cost_estimate=pl.CostEstimate(flops=8 << 30, bytes_accessed=8 << 20, transcendentals=0),
@@ -442,10 +469,10 @@
         upper_inv,
         lower_inv,
         solution.reshape(1, B),
-        right_side.reshape(4, B),
+        right_side,
         diagonal_block_inverses.reshape(B, B),
     )
-    return updated.reshape(matrix.shape), residual.reshape(right_side.shape), precond
+    return updated.reshape(matrix.shape), residual, precond
 
 
 def solution(mesh):

time: 107 us -> 91.3 us (0.85)
  the two profiles are of different devices: /device:TPU:44 before, /device:TPU:129 now
where the time goes in v2:
time: 91.3 us; the launch traced here: 91.1 us
  Pallas kernels  86.2 us (94%)
  local copies, waits for them, and re-layouts  4.27 us (5%)
    pallas_call x1, Pallas kernels, shards(): pl.pallas_call(kernel, out_shape=(jax.ShapeDtypeStruct((4 * B, B), bf16),...  86.2 us
    unnamed x7, local copies, waits for them, and re-layouts  4.27 us

profile of v2, /device:TPU:129, one launch (start us, length us, event | category | flops | bytes accessed | tf_op | source)
XLA Modules:
  0.0 91.1 jit_solution(2803978479563360276)
XLA Ops:
  0.6 86.2 %shard_map.85 = (bf16[2048,512]{1,0:T(8,128)(2,1)}, f32[4,1,512]{2,1,0:T(1,128)}, f32[8,512]{1,0:T(8,128)}) custom-call(bf16[2048,512]{1,0:T(8,128)(2,1)} %bitcast.7, bf16[2,512,512]{2,1,0:T(8,128)(2,1)} %u_hbm.1, bf16[2,512,512]{2,1,0:T(8,128)(2,1)} %l_hbm.1, bf16[1,512]{1,0:T(2,128)(2,1)} %bitcast.9, f32[4,1,512]{2,1,0:T(1,128)} %rhs_ref.1, ...), custom_call_target="tpu_custom_call" | custom-call | flops 8589934592 | bytes 8388608 | tf_op jit(solution)/shard_map/pallas_call | solution.py:447
  86.9 0.0 copy-start.1
  86.9 0.0 copy-start
  86.9 3.1 %copy.13 = bf16[4,1,512,1,1,512]{5,2,4,3,1,0:T(8,128)(2,1)} copy(bf16[4,1,512,1,1,512]{5,2,4,3,1,0:T(8,128)(2,1)} %bitcast.6) | data formatting | bytes 4194304
  89.9 0.0 copy-done.1
  89.9 0.6 copy.14
  90.5 0.0 copy-done
  90.5 0.6 copy.15
Async XLA Ops:
  86.9 3.1 %copy-start.1 = (f32[4,1,512]{2,1,0:T(1,128)S(1)}, f32[4,1,512]{2,1,0:T(1,128)}, u32[]{:S(2)}) copy-start(f32[4,1,512]{2,1,0:T(1,128)} %get-tuple-element.16) | copy-start | bytes 24580
  86.9 3.7 %copy-start = (f32[8,512]{1,0:T(8,128)S(1)}, f32[8,512]{1,0:T(8,128)}, u32[]{:S(2)}) copy-start(f32[8,512]{1,0:T(8,128)} %get-tuple-element.17) | copy-start | bytes 49156

commit v3 on v2

--- a/solution.py
+++ b/solution.py
@@ -9,29 +9,30 @@
 B = 512
 CH = 64
 CR = 16
-NPOS = 3
-NC = B // CH + 1
+ND = B // CH
 DIRS = ((1, 0), (-1, 0), (0, 1), (0, -1))
 TABLE = (
     (
-        (2049, 221261, 184641, 147824, 27936, 217255, 151904, 95728, 53056, 69879, 246113, 115112, 85856, 229655, 145761, 101824, 109488, 141619, 190849, 141760, 125360, 198994, 254353, 158160, 182576, 229643, 205177, 254356, 237984, 229563, 194432, 254432),
-        (1032, 237952, 66900, 64752, 164736, 254416, 205191, 117664, 188728, 156096, 138720, 126928, 196872, 229736, 181696, 131864, 237786, 246056, 173400, 140042, 213163, 229657, 152932, 120768, 147563, 155828, 126448, 112544, 82506, 106788, 221364, 70310),
+        (65537, 183240781, 148513089, 122168688, 34446624, 174723751, 122299232, 78557680, 52027712, 60954871, 200811361, 104343976, 78242656, 191896855, 122102625, 87141824, 95775664, 121970483, 157099905, 121974208, 104672176, 165749586, 209463697, 130887120, 148447024, 191896331, 174335353, 209463700, 192162208, 191894203, 157214592, 209465312),
+        (32776, 192161664, 69247828, 60791024, 139487104, 209464784, 174335879, 104425888, 157032248, 130821568, 121876448, 113110480, 165681928, 191898472, 148417984, 121658648, 192157402, 200810280, 148153176, 121920266, 174592683, 191896857, 122332004, 104525248, 122162283, 130814644, 104706544, 95873440, 78137418, 95690020, 183243956, 69358246),
     ),
     (
-        (205006, 2050, 147856, 201010, 151799, 11104, 62448, 152016, 78087, 44896, 156056, 196962, 254247, 69424, 93040, 129330, 158019, 85376, 133552, 190834, 207185, 141808, 158160, 229730, 213259, 158016, 197012, 229722, 221435, 172368, 246192, 210768),
-        (123360, 520, 23360, 74660, 205248, 124352, 60896, 229815, 147952, 139528, 85984, 121792, 246120, 155880, 99624, 140224, 205128, 213177, 140553, 181048, 254218, 180395, 128848, 168772, 180388, 163947, 71552, 117728, 164068, 82969, 62613, 196916),
+        (174331086, 65538, 122169744, 165814066, 122296567, 17130336, 60715504, 122301904, 69606151, 43377504, 130820504, 165684066, 209460519, 60940080, 78472560, 104800050, 130883907, 78227328, 113322928, 157099378, 174400337, 121975280, 130887120, 191898978, 182983435, 130883904, 165685652, 191898458, 183245051, 148120400, 200813488, 174515024),
+        (104607712, 16392, 25911616, 69495204, 174337472, 104639936, 60665824, 191900599, 122171888, 121903880, 78245856, 104558016, 200811368, 130816232, 87072040, 121925056, 174334280, 174593209, 121936649, 148397880, 209459978, 148378283, 104784720, 139616580, 148378276, 139463787, 69396352, 104427488, 139466980, 78152729, 60723349, 165682996),
     ),
 )
 ROOT_DIR = ((0, 2, 3, 1), (1, 2, 3, 0))
-LAG_MAX = 31
+NPOS = 3
 EY = 2
 EZ = 7
-EX = 15
-EC = (8, 10, 13, 16, 19, 21, 24, 27)
-EF0 = 30
-EF1 = 33
-EP = 99
-EW = 99
+EX = 13
+EC = 8
+ECS = 3
+EF0 = 31
+EF1 = 34
+PD = 9
+PW = 2
+LAST = 39
 f32, bf16 = jnp.float32, jnp.bfloat16
 
 
@@ -140,9 +141,13 @@
             for k in range(32):
                 word = jnp.where(q == k, jnp.int32(TABLE[r][h][k]), word)
             for t in range(2):
-                v = (word // (512**t)) % 512
-                mask = v % 16
-                info.append((r, 2 * h + t, v // 16, [(mask // (1 << d)) % 2 for d in range(4)]))
+                v = (word // (16384**t)) % 16384
+                kids = [(v // (1 << d)) % 2 for d in range(4)]
+                info.append((r, 2 * h + t, (v // 16) % 32, v // 512, kids))
+    com_tick = jnp.int32(0)
+    for r, t, lg, clg, kids in info:
+        com_tick = jnp.maximum(com_tick, clg + 1)
+    w_tick = jnp.maximum(com_tick + PD + PW, EX + 1)
     nbr = [at(dy, dz) for dy, dz in DIRS]
     for r in range(2):
         pl.when(q == r)(lambda r=r: pltpu.make_async_copy(a_hbm, strm.at[r, pl.ds(0, 4 * B)], s_loc.at[4]).wait())
@@ -151,12 +156,12 @@
     pl.semaphore_wait(bar, 17 + jnp.where(is_q, 2, jnp.where((q == 5) | (q == 6), 1, 0)))
 
     def hop(r, t, n, d):
-        part = strm.at[r, pl.ds(pl.multiple_of(B * t + CH * jnp.where(n > NPOS, n - 1, n), CH), CH)]
+        part = strm.at[r, pl.ds(pl.multiple_of(B * t + CH * n, CH), CH)]
         return rcopy(part, part, s_send.at[r, t, d], s_recv.at[r, t, n], (p, nbr[d]))
 
     def com_hop(r, t, d):
         part = strm.at[r, pl.ds(4 * B + CR * t, CR)]
-        return rcopy(part, part, s_send.at[r, t, d], s_recv.at[r, t, NPOS], (p, nbr[d]))
+        return rcopy(part, part, s_send.at[r, t, d], s_recv.at[r, t, ND], (p, nbr[d]))
 
     def inject(lo, hi):
         for r in range(2):
@@ -189,10 +194,11 @@
         com_own().wait()
 
     def blk_copy(j):
-        return rcopy(a_v.at[pl.ds(0, B)], chb.at[j - 1], s_blks, s_blkr.at[j - 1], (p, 0))
+        return rcopy(a_v.at[pl.ds(0, B)], chb.at[j], s_blks, s_blkr.at[j], (p, 0))
 
     for j in range(1, 7):
         pl.when((q == j) & (p > j))(lambda j=j: blk_copy(j).start())
+    pl.when(is_q & (p > 0))(lambda: pltpu.make_async_copy(a_hbm.at[pl.ds(0, B)], chb.at[0], s_blkr.at[0]).start())
 
     def xb_copy(o):
         return rcopy(xb.at[core], xb.at[core], s_xsend.at[o], s_prim, (2 * (o + 1) + core, q))
@@ -207,27 +213,22 @@
         for o in (0, 2, 1):
             xb_copy(o).start()
 
-    def ticks(lo, hi):
-        def one(k, c):
-            for r, t, lg, kids in info:
-                n = k - lg
-                other = q != r
-
-                @pl.when((n >= 0) & (n < NC) & (n != NPOS) & other)
-                def _():
-                    hop(r, t, n, 0).wait_recv()
-                    for d in range(4):
-                        pl.when(kids[d] == 1)(lambda d=d: hop(r, t, n, d).start())
-
-                @pl.when((n == NPOS) & other)
-                def _():
-                    com_hop(r, t, 0).wait_recv()
-                    for d in range(4):
-                        pl.when(kids[d] == 1)(lambda d=d: com_hop(r, t, d).start())
-
-            return c
-
-        lax.fori_loop(lo, hi, one, 0)
+    def streams(k):
+        for r, t, lg, clg, kids in info:
+            n = k - lg
+            other = q != r
+
+            @pl.when((n >= 0) & (n < ND) & other)
+            def _():
+                hop(r, t, n, 0).wait_recv()
+                for d in range(4):
+                    pl.when(kids[d] == 1)(lambda d=d: hop(r, t, n, d).start())
+
+            @pl.when((k == clg) & other)
+            def _():
+                com_hop(r, t, 0).wait_recv()
+                for d in range(4):
+                    pl.when(kids[d] == 1)(lambda d=d: com_hop(r, t, d).start())
 
     def rz_copy(o):
         return rcopy(rz.at[z], rz.at[z], s_rzs.at[o], s_rzr.at[z], (p, zm[o]))
@@ -263,17 +264,13 @@
     def ev_c(j):
         @pl.when(is_q & (p > j))
         def _():
-            blk = a_v.at[pl.ds(0, B)] if j == 0 else chb.at[j - 1]
-            if j:
-                rcopy(a_v.at[pl.ds(0, B)], chb.at[j - 1], s_blks, s_blkr.at[j - 1], ((p + 1) % 8, 0)).wait_recv()
+            rcopy(a_v.at[pl.ds(0, B)], chb.at[j], s_blks, s_blkr.at[j], ((p + 1) % 8, 0)).wait_recv()
             x_recv(j)
             row = row_of(xs[j, 0:4, :]).astype(bf16)
-            acc[0:1, :] = acc[0:1, :] - dot_t(jnp.broadcast_to(row, (16, B)), blk[...])[0:1, :]
+            acc[0:1, :] = acc[0:1, :] - dot_t(jnp.broadcast_to(row, (16, B)), chb[j])[0:1, :]
 
         @pl.when(is_q & (p == j))
         def _():
-            if j == 0:
-                pass
             s = acc[0:1, :]
             hi = s.astype(bf16).astype(f32)
             mid = (s - hi).astype(bf16).astype(f32)
@@ -363,27 +360,27 @@
         v1 = dot(u_v[0], dot(l_v[0], comf[1]).astype(bf16)).astype(bf16)
         w_v[0] = (v - dot(v1, w1)).astype(bf16)
 
-    last = NC + LAG_MAX
-    events = [(0, lambda: com_ready()), (EY, ev_y), (EZ, ev_z), (EX, ev_x), (EF0, ev_f0), (EF1, ev_f1)]
-    events += [(EC[j], lambda j=j: ev_c(j)) for j in range(8)]
-    events += [(NPOS + 1 + LAG_MAX, ev_com), (EP, ev_pair), (EW, ev_w)]
-
     def com_ready():
         for r in range(2):
             pl.when((q == r) & jnp.logical_not(src_com))(lambda r=r: com_copy(0).wait_recv())
         for r in range(2):
             pl.when(q == r)(lambda r=r: [com_hop(r, t, ROOT_DIR[r][t]).start() for t in range(4)] and None)
-        inject(NPOS + 1, NC)
-
-    now = 0
-    for when, ev in sorted(events, key=lambda e: e[0]):
-        when = min(when, last)
-        if when > now:
-            ticks(now, when)
-            now = when
-        ev()
-    if now < last:
-        ticks(now, last)
+        inject(NPOS, ND)
+
+    com_ready()
+    events = ((EY, ev_y), (EZ, ev_z), (EX, ev_x), (EF0, ev_f0), (EF1, ev_f1))
+
+    def tick(k, c):
+        for when, ev in events:
+            pl.when(k == when)(ev)
+        pl.when((k >= EC) & ((k - EC) % ECS == 0) & (k < EC + 8 * ECS))(lambda: ev_c((k - EC) // ECS))
+        pl.when(k == com_tick)(ev_com)
+        pl.when(k == com_tick + PD)(ev_pair)
+        pl.when(k == w_tick)(ev_w)
+        streams(k)
+        return c
+
+    lax.fori_loop(0, LAST, tick, 0)
 
     def step(s, c):
         i256 = pl.ds(pl.multiple_of(s * 256, 256), 256)
@@ -395,7 +392,7 @@
     lax.fori_loop(0, 8, step, 0)
     ev_f2()
 
-    for r, t, lg, kids in info:
+    for r, t, lg, clg, kids in info:
         for d in range(4):
             sent = strm.at[r, pl.ds(0, B + CR)]
             pl.when(kids[d] == 1)(
@@ -455,11 +452,11 @@
         out_specs=(hbm, vmem, vmem),
         scratch_shapes=[
             vm((4 * B, B), bf16), vm((2, 4 * B + 64, B), bf16), vm((2, B, B), bf16), vm((2, B, B), bf16),
-            vm((B, B), bf16), vm((6, B, B), bf16), vm((2, B, B), bf16), vm((2, B, B), bf16), vm((2, B, B), bf16),
+            vm((B, B), bf16), vm((7, B, B), bf16), vm((2, B, B), bf16), vm((2, B, B), bf16), vm((2, B, B), bf16),
             vm((B, B), f32), vm((4, 16, 128), f32), vm((8, 16, 128), f32), vm((8, 8, 128), f32), vm((32, 128), f32), vm((8, B), f32),
             vm((4 * B, B), bf16),
-            dma((7,)), dma, dma((2, 4, 4)), dma((2, 4, NC)), dma((4,)), dma, dma, dma((7,)), dma,
-            dma, dma((6,)), dma((3,)), dma((4,)), dma((7,)), dma((8,)), dma((8,)), dma((8,)), dma((10,)), dma, dma,
+            dma((7,)), dma, dma((2, 4, 4)), dma((2, 4, ND + 1)), dma((4,)), dma, dma, dma((7,)), dma,
+            dma, dma((7,)), dma((3,)), dma((4,)), dma((7,)), dma((8,)), dma((8,)), dma((8,)), dma((10,)), dma, dma,
             dma((2,)), dma((2,)), dma((2, 3)), dma((2, 4)),
         ],
         compiler_params=pltpu.CompilerParams(collective_id=0, has_side_effects=True, vmem_limit_bytes=56 << 20),

time: 91.3 us -> 88.3 us (0.967)
  the two profiles are of different devices: /device:TPU:129 before, /device:TPU:135 now
where the time goes in v3:
time: 88.3 us; the launch traced here: 88.1 us
  Pallas kernels  83.2 us (94%)
  local copies, waits for them, and re-layouts  4.27 us (5%)
    pallas_call x1, Pallas kernels, shards(): pl.pallas_call(kernel, out_shape=(jax.ShapeDtypeStruct((4 * B, B), bf16),...  83.2 us
    unnamed x7, local copies, waits for them, and re-layouts  4.27 us

profile of v3, /device:TPU:135, one launch (start us, length us, event | category | flops | bytes accessed | tf_op | source)
XLA Modules:
  0.0 88.1 jit_solution(6544120018338917108)
XLA Ops:
  0.6 83.2 %shard_map.85 = (bf16[2048,512]{1,0:T(8,128)(2,1)}, f32[4,1,512]{2,1,0:T(1,128)}, f32[8,512]{1,0:T(8,128)}) custom-call(bf16[2048,512]{1,0:T(8,128)(2,1)} %bitcast.7, bf16[2,512,512]{2,1,0:T(8,128)(2,1)} %u_hbm.1, bf16[2,512,512]{2,1,0:T(8,128)(2,1)} %l_hbm.1, bf16[1,512]{1,0:T(2,128)(2,1)} %bitcast.9, f32[4,1,512]{2,1,0:T(1,128)} %rhs_ref.1, ...), custom_call_target="tpu_custom_call" | custom-call | flops 8589934592 | bytes 8388608 | tf_op jit(solution)/shard_map/pallas_call | solution.py:444
  83.8 0.0 copy-start.1
  83.8 0.0 copy-start
  83.9 3.1 %copy.13 = bf16[4,1,512,1,1,512]{5,2,4,3,1,0:T(8,128)(2,1)} copy(bf16[4,1,512,1,1,512]{5,2,4,3,1,0:T(8,128)(2,1)} %bitcast.6) | data formatting | bytes 4194304
  86.9 0.0 copy-done.1
  86.9 0.6 copy.14
  87.5 0.0 copy-done
  87.5 0.6 copy.15
Async XLA Ops:
  83.8 3.1 %copy-start.1 = (f32[4,1,512]{2,1,0:T(1,128)S(1)}, f32[4,1,512]{2,1,0:T(1,128)}, u32[]{:S(2)}) copy-start(f32[4,1,512]{2,1,0:T(1,128)} %get-tuple-element.16) | copy-start | bytes 24580
  83.8 3.7 %copy-start = (f32[8,512]{1,0:T(8,128)S(1)}, f32[8,512]{1,0:T(8,128)}, u32[]{:S(2)}) copy-start(f32[8,512]{1,0:T(8,128)} %get-tuple-element.17) | copy-start | bytes 49156

commit v4 on v3

--- a/solution.py
+++ b/solution.py
@@ -25,12 +25,12 @@
 NPOS = 3
 EY = 2
 EZ = 7
-EX = 13
+EX = 11
 EC = 8
 ECS = 3
 EF0 = 31
 EF1 = 34
-PD = 9
+PD = 10
 PW = 2
 LAST = 39
 f32, bf16 = jnp.float32, jnp.bfloat16
@@ -435,6 +435,20 @@
             fy_copy(o).wait_send()
 
     pltpu.make_async_copy(out_v, out_hbm, s_out).wait()
+
+
+def hand_out(a_hbm, res_in, pre_in, out_hbm, res_out, pre_out, buf, res_v, pre_v, s_in, s_out):
+    steps = [(a_hbm.at[w], buf.at[w], out_hbm.at[w]) for w in (pl.ds(256 * k, 256) for k in range(8))]
+    steps = [(res_in, res_v, res_out), (pre_in, pre_v, pre_out)] + steps
+    ins = [pltpu.make_async_copy(a, b, s_in.at[k]) for k, (a, b, c) in enumerate(steps)]
+    outs = [pltpu.make_async_copy(b, c, s_out.at[k]) for k, (a, b, c) in enumerate(steps)]
+    for c in ins:
+        c.start()
+    for c, o in zip(ins, outs):
+        c.wait()
+        o.start()
+    for o in outs:
+        o.wait()
 
 
 def shards(matrix, upper_inv, lower_inv, solution, right_side, diagonal_block_inverses):
@@ -469,6 +483,19 @@
         right_side,
         diagonal_block_inverses.reshape(B, B),
     )
+    updated, residual, precond = pl.pallas_call(
+        hand_out,
+        out_shape=(
+            jax.ShapeDtypeStruct((4 * B, B), bf16),
+            jax.ShapeDtypeStruct((4, 1, B), f32),
+            jax.ShapeDtypeStruct((8, B), f32),
+        ),
+        in_specs=[hbm, hbm, hbm],
+        out_specs=(hbm, hbm, hbm),
+        scratch_shapes=[vm((4 * B, B), bf16), vm((4, 1, B), f32), vm((8, B), f32), dma((10,)), dma((10,))],
+        compiler_params=pltpu.CompilerParams(vmem_limit_bytes=60 << 20),
+        cost_estimate=pl.CostEstimate(flops=0, bytes_accessed=4 << 20, transcendentals=0),
+    )(updated, residual, precond)
     return updated.reshape(matrix.shape), residual, precond
 
 

time: 88.3 us -> 86.6 us (0.981)
  local copies, waits for them, and re-layouts: 4.27 us -> 0 us
  Pallas kernels: 83.2 us -> 85.7 us
    unnamed x7 -> x0, local copies, waits for them, and re-layouts: 4.27 us -> none
    pallas_call x0 -> x1, Pallas kernels: none -> 2.46 us  [shards(): pl.pallas_call(hand_out, out_shape=(jax.ShapeDtypeStruct((4 * B, B), bf16...]
where the time goes in v4:
time: 86.6 us; the launch traced here: 86.3 us
  Pallas kernels  85.7 us (99%)
    pallas_call x1, Pallas kernels, shards(): pl.pallas_call(kernel, out_shape=(jax.ShapeDtypeStruct((4 * B, B), bf16),...  83.2 us
    pallas_call x1, Pallas kernels, shards(): pl.pallas_call(hand_out, out_shape=(jax.ShapeDtypeStruct((4 * B, B), bf16...  2.46 us

profile of v4, /device:TPU:135, one launch (start us, length us, event | category | flops | bytes accessed | tf_op | source)
XLA Modules:
  0.0 86.3 jit_solution(1083832252108026460)
XLA Ops:
  0.6 83.2 %shard_map.85 = (bf16[2048,512]{1,0:T(8,128)(2,1)}, f32[4,1,512]{2,1,0:T(1,128)}, f32[8,512]{1,0:T(8,128)}) custom-call(bf16[2048,512]{1,0:T(8,128)(2,1)} %bitcast.6, bf16[2,512,512]{2,1,0:T(8,128)(2,1)} %u_hbm.1, bf16[2,512,512]{2,1,0:T(8,128)(2,1)} %l_hbm.1, bf16[1,512]{1,0:T(2,128)(2,1)} %bitcast.9, f32[4,1,512]{2,1,0:T(1,128)} %rhs_ref.1, ...), custom_call_target="tpu_custom_call" | custom-call | flops 8589934592 | bytes 8388608 | tf_op jit(solution)/shard_map/pallas_call | solution.py:458
  83.9 2.5 %shard_map.86 = (bf16[2048,512]{1,0:T(8,128)(2,1)}, f32[4,1,512]{2,1,0:T(1,128)}, f32[8,512]{1,0:T(8,128)}) custom-call(bf16[2048,512]{1,0:T(8,128)(2,1)} %get-tuple-element.9.a_hbm, f32[4,1,512]{2,1,0:T(1,128)} %get-tuple-element.10.res_in, f32[8,512]{1,0:T(8,128)} %get-tuple-element.11.pre_in), custom_call_target="tpu_custom_call" | custom-call | bytes 4194304 | tf_op jit(solution)/shard_map/pallas_call | solution.py:486

commit v5 on v4

--- a/solution.py
+++ b/solution.py
@@ -22,7 +22,7 @@
     ),
 )
 ROOT_DIR = ((0, 2, 3, 1), (1, 2, 3, 0))
-NPOS = 3
+NPOS = 2
 EY = 2
 EZ = 7
 EX = 11
@@ -383,13 +383,13 @@
     lax.fori_loop(0, LAST, tick, 0)
 
     def step(s, c):
-        i256 = pl.ds(pl.multiple_of(s * 256, 256), 256)
+        i256 = pl.ds(pl.multiple_of(s * B, B), B)
         prod = dot(strm[0, i256], w_v[0]) + dot(strm[1, i256], w_v[1])
         out_v[i256] = (a_v[i256].astype(f32) - prod).astype(bf16)
         pltpu.make_async_copy(out_v.at[i256], out_hbm.at[i256], s_out).start()
         return c
 
-    lax.fori_loop(0, 8, step, 0)
+    lax.fori_loop(0, 4, step, 0)
     ev_f2()
 
     for r, t, lg, clg, kids in info:

time: 86.6 us -> 86.1 us (level)
  no operation moved by 1% of the time
where the time goes in v5:
time: 86.1 us; the launch traced here: 85.8 us
  Pallas kernels  85.2 us (99%)
    pallas_call x1, Pallas kernels, shards(): pl.pallas_call(kernel, out_shape=(jax.ShapeDtypeStruct((4 * B, B), bf16),...  82.7 us
    pallas_call x1, Pallas kernels, shards(): pl.pallas_call(hand_out, out_shape=(jax.ShapeDtypeStruct((4 * B, B), bf16...  2.46 us

profile of v5, /device:TPU:135, one launch (start us, length us, event | category | flops | bytes accessed | tf_op | source)
XLA Modules:
  0.0 85.8 jit_solution(16624161090724648391)
XLA Ops:
  0.6 82.7 %shard_map.85 = (bf16[2048,512]{1,0:T(8,128)(2,1)}, f32[4,1,512]{2,1,0:T(1,128)}, f32[8,512]{1,0:T(8,128)}) custom-call(bf16[2048,512]{1,0:T(8,128)(2,1)} %bitcast.6, bf16[2,512,512]{2,1,0:T(8,128)(2,1)} %u_hbm.1, bf16[2,512,512]{2,1,0:T(8,128)(2,1)} %l_hbm.1, bf16[1,512]{1,0:T(2,128)(2,1)} %bitcast.9, f32[4,1,512]{2,1,0:T(1,128)} %rhs_ref.1, ...), custom_call_target="tpu_custom_call" | custom-call | flops 8589934592 | bytes 8388608 | tf_op jit(solution)/shard_map/pallas_call | solution.py:458
  83.4 2.5 %shard_map.86 = (bf16[2048,512]{1,0:T(8,128)(2,1)}, f32[4,1,512]{2,1,0:T(1,128)}, f32[8,512]{1,0:T(8,128)}) custom-call(bf16[2048,512]{1,0:T(8,128)(2,1)} %get-tuple-element.9.a_hbm, f32[4,1,512]{2,1,0:T(1,128)} %get-tuple-element.10.res_in, f32[8,512]{1,0:T(8,128)} %get-tuple-element.11.pre_in), custom_call_target="tpu_custom_call" | custom-call | bytes 4194304 | tf_op jit(solution)/shard_map/pallas_call | solution.py:486
